TPU v7x, 32 devices: a whole 2x2x4 slice. The times are simulated.
32 devices in a mesh: grp: 2 (over y), blk: 8 (over z, x), pair: 2 (over core).
Axes of the slice: x: 2, y: 2, z: 4, core: 2. Of those that a mesh axis runs over, the one named last changes fastest.
Arguments:
- wavefunc: bfloat16 [96, 16, 2, 768], P(('grp', 'blk')), parts along dimension 0, may hold values from -6 to 6
- haydock: float32 [96, 128], P(('grp', 'blk')), parts along dimension 0, may hold values from -6 to 6
- screened: bfloat16 [16, 768, 768], P(('grp', 'blk')), parts along dimension 0, may hold values from -0.21875 to 0.21875
- coulomb: float32 [1536], P('grp'), parts along dimension 0, may hold values from 0.05 to 1
- umklapp_map: int32 [3, 768], replicated, may hold values from 0 to 767, each once within a row
Outputs:
- kernel_out: float32 [96, 128], P(('grp', 'blk')), parts along dimension 0
There are 2 independent parts, one for each index of `grp`. A program takes and returns all parts, laid end to end along the dimension named above; an argument that names none is the same for every part. Nothing has to cross between parts.
Inputs may be any that keep to these rules, and one draw needn't show every extreme that they name: Each row of umklapp_map is a permutation of 0 .. 767.
All inputs are finite; a program needn't handle non-finite values.
Results may differ from a plain program's by a relative error of at most 0.015.
Values may be sent and summed in bfloat16 or wider, within the bound.
A program may use at most 64 MiB of HBM per device.

v0:
```python
import functools
import math

import jax
import jax.numpy as jnp
from jax import lax
from jax.experimental import pallas as pl
from jax.experimental.pallas import tpu as pltpu
from jax.sharding import PartitionSpec as P

NV = 8
NC = 8
STOPS = 2
MESH = pl.DeviceIdType.MESH
NT = (((1,), (1,)), ((), ()))


def dot_nt(a, b):
    return lax.dot_general(a, b, NT, preferred_element_type=jnp.float32)


def dot_nn(a, b):
    return jnp.dot(a, b, preferred_element_type=jnp.float32)


def make_pieces(wave, hay):
    count, bands, _, planes = wave.shape
    rows = wave.reshape(count, 2, NV, 2, planes).transpose(1, 3, 0, 2, 4)
    rows = rows.reshape(2, 2 * count * NV, planes)
    psi = hay.reshape(count, 2, NV, NC).transpose(1, 0, 3, 2)
    eye = jnp.eye(count, dtype=jnp.float32)
    wide = (psi[:, :, :, None, :] * eye[None, :, None, :, None]).reshape(2, count * NC, count * NV)
    top = jnp.concatenate([wide[0], -wide[1]], axis=1)
    low = jnp.concatenate([wide[1], wide[0]], axis=1)
    mix = jnp.concatenate([top, low], axis=0).astype(jnp.bfloat16)
    return rows, mix


def unpack_result(total, count):
    half = count * NC
    out_re = total[:NV, :half] - total[NV:, half : 2 * half]
    out_im = total[NV:, :half] + total[:NV, half : 2 * half]
    out = jnp.stack([out_re, out_im]).reshape(2, NV, count, NC)
    return out.transpose(2, 0, 1, 3).reshape(count, 2 * NV * NC)


def fold_rows(f_rows, cond, count):
    t = dot_nt(f_rows, cond)
    rows, lanes = t.shape
    keep = (lax.broadcasted_iota(jnp.int32, t.shape, 0) // NV) % count == (
        lax.broadcasted_iota(jnp.int32, t.shape, 1) // NC
    ) % count
    t = jnp.where(keep, t, 0.0).reshape(2, count, NV, lanes)
    return jnp.sum(t, axis=1).reshape(2 * NV, lanes)


def kernel(
    count, scale_d, scale_x,
    piece_ref, weight_ref, map_ref, coul_ref, out_ref,
    ubuf, sel, fbuf, stage, res, xbuf,
    recv_near, recv_peer, send_piece, send_res, recv_res, send_x, recv_x,
):
    grp = lax.axis_index("grp")
    me = lax.axis_index("blk")
    p = lax.axis_index("pair")
    blocks = lax.axis_size("blk")
    z = me // 2
    x = me % 2
    worker = me < STOPS + 1
    planes = weight_ref.shape[0]
    half = planes // 2
    edge = count * NV

    barrier = pltpu.get_barrier_semaphore()
    for d in range(1, 2 * blocks):
        other = (me * 2 + p + d) % (2 * blocks)
        pl.semaphore_signal(barrier, inc=1, device_id=(grp, other // 2, other % 2), device_id_type=MESH)
    ubuf[me] = piece_ref[...]
    pl.semaphore_wait(barrier, 2 * blocks - 1)

    def routes(b):
        zb = b // 2
        xb = b % 2
        return (
            (worker & (b != me), me, 1 - p, recv_peer),
            ((z >= 1) & (xb == x) & (zb >= z), me - 2, p, recv_near),
            (((z == 0) & (xb == x)) | ((me == 3) & (xb == 1) & (zb >= 1)), me + 1 - 2 * x, p, recv_near),
            ((me == 0) & (b < 2), me + 2, p, recv_near),
        )

    def copy_of(b, kind, target, core, sems):
        return pltpu.make_async_remote_copy(
            src_ref=ubuf.at[b, p],
            dst_ref=ubuf.at[b, p],
            send_sem=send_piece.at[kind, b],
            recv_sem=sems.at[b],
            device_id=(grp, target, core),
            device_id_type=MESH,
        )

    def forward(b):
        for kind, (go, target, core, sems) in enumerate(routes(b)):
            @pl.when(go)
            def _():
                copy_of(b, kind, target, core, sems).start()

    def drain(b):
        for kind, (go, target, core, sems) in enumerate(routes(b)):
            @pl.when(go)
            def _():
                copy_of(b, kind, target, core, sems).wait_send()

    def arrive(b):
        pltpu.make_async_copy(ubuf.at[b, p], ubuf.at[b, p], recv_near.at[b]).wait()
        forward(b)

    def arrive_peer(b):
        pltpu.make_async_copy(ubuf.at[b, 1 - p], ubuf.at[b, 1 - p], recv_peer.at[b]).wait()

    forward(me)

    cond_own = piece_ref[1, :, :planes].astype(jnp.float32)
    amp = dot_nn(piece_ref[0, :, planes : planes + 2 * edge], piece_ref[0, :, :planes])
    c_re, c_im = cond_own[:edge], cond_own[edge:]
    a_re, a_im = amp[:edge], amp[edge:]
    xbuf[me, 0:1, :] = jnp.sum(c_re * a_re + c_im * a_im, axis=0, keepdims=True)
    xbuf[me, 1:2, :] = jnp.sum(c_re * a_im - c_im * a_re, axis=0, keepdims=True)

    def x_copy(d):
        return pltpu.make_async_remote_copy(
            src_ref=xbuf.at[me],
            dst_ref=xbuf.at[me],
            send_sem=send_x.at[d],
            recv_sem=recv_x.at[me],
            device_id=(grp, (me + d) % blocks, p),
            device_id_type=MESH,
        )

    for d in range(1, blocks):
        x_copy(d).start()

    def res_copy(b, core):
        return pltpu.make_async_remote_copy(
            src_ref=stage.at[b],
            dst_ref=res.at[me * 2 + p],
            send_sem=send_res.at[b, core],
            recv_sem=recv_res.at[me * 2 + p],
            device_id=(grp, b, core),
            device_id_type=MESH,
        )

    @pl.when(worker)
    def _():
        s = me
        base = pl.multiple_of(p * half, 128)
        sel[...] = jnp.where(
            map_ref[...] == lax.broadcasted_iota(jnp.int32, (planes, planes), 1), 1.0, 0.0
        ).astype(jnp.bfloat16)

        def step(t, carry):
            i = jnp.where(s == 2, (t + 2) % blocks, t)
            b = (i + s) % blocks
            first = jnp.where((s == 1) & (t == 0), 0, b)
            take = ((s == 0) & (t >= 1)) | ((s == 1) & (t <= 6)) | ((s == 2) & (t <= 5))
            more = (s == 2) & (t == 1)

            @pl.when(more)
            def _():
                arrive(3)

            @pl.when(take)
            def _():
                arrive(first)
                arrive_peer(first)

            @pl.when(more)
            def _():
                arrive_peer(3)

            val_j = ubuf[i, 0, :, :planes]
            mix_j = ubuf[i, 0, :, planes : planes + 2 * edge]
            amp_j = dot_nn(mix_j, val_j).astype(jnp.bfloat16)
            perm = dot_nt(amp_j, sel[...])
            perm_re = perm.astype(jnp.bfloat16)
            perm_im = jnp.concatenate([perm[edge:], -perm[:edge]], axis=0).astype(jnp.bfloat16)
            cond_t = dot_nt(sel[pl.ds(base, half), :], ubuf[i, 1, :, :planes]).astype(jnp.bfloat16)
            val_b = ubuf[b, 0, :, :planes]
            tile = 128
            for r in range(half // tile):
                rows = pl.ds(pl.multiple_of(base + r * tile, 128), tile)
                w = weight_ref[rows, :].astype(jnp.float32)
                left = cond_t[r * tile : (r + 1) * tile]
                h_re = (dot_nn(left, perm_re) * w).astype(jnp.bfloat16)
                h_im = (dot_nn(left, perm_im) * w).astype(jnp.bfloat16)
                g_re = dot_nt(val_b, h_re)
                g_im = dot_nt(val_b, h_im)
                f_re = g_re[:edge] + g_im[edge:]
                f_im = g_im[:edge] - g_re[edge:]
                fbuf[:, r * tile : (r + 1) * tile] = (
                    jnp.concatenate([f_re, f_im], axis=0) * scale_d
                ).astype(jnp.bfloat16)
            cond_b = ubuf[b, 1, :, pl.ds(base, half)]
            part = fold_rows(fbuf[...], cond_b, count)
            stage[b, :, : 2 * edge] = part
            for core in range(2):
                mine = (b == me) & (p == core)

                @pl.when(mine)
                def _():
                    res[me * 2 + p, :, : 2 * edge] = part

                @pl.when(jnp.logical_not(mine))
                def _():
                    res_copy(b, core).start()

            return carry

        lax.fori_loop(0, blocks, step, 0)

    @pl.when(jnp.logical_not(worker))
    def _():
        for b in range(3, blocks):
            @pl.when((b % 2 == x) & (b // 2 > z))
            def _():
                arrive(b)

    for d in range(1, blocks):
        src = (me + d) % blocks
        pltpu.make_async_copy(xbuf.at[src], xbuf.at[src], recv_x.at[src]).wait()
    y = jnp.sum(xbuf[...], axis=0) * coul_ref[...] * scale_x
    y_re, y_im = y[0:1], y[1:2]
    v_re = piece_ref[0, :edge, :planes].astype(jnp.float32)
    v_im = piece_ref[0, edge:, :planes].astype(jnp.float32)
    f_rows = jnp.concatenate([y_re * v_re + y_im * v_im, y_im * v_re - y_re * v_im], axis=0)
    total = fold_rows(f_rows.astype(jnp.bfloat16), piece_ref[1, :, :planes], count)

    for slot in range(2 * (STOPS + 1)):
        @pl.when(slot != me * 2 + p)
        def _():
            pltpu.make_async_copy(res.at[slot], res.at[slot], recv_res.at[slot]).wait()
    for slot in range(2 * (STOPS + 1)):
        total = total + res[slot, :, : 2 * edge]
    out_ref[...] = total

    for b in range(blocks):
        @pl.when(worker | ((b % 2 == x) & (b // 2 >= z)))
        def _():
            drain(b)
    for d in range(1, blocks):
        x_copy(d).wait_send()

    @pl.when(worker)
    def _():
        for b in range(blocks):
            for core in range(2):
                @pl.when(jnp.logical_not((b == me) & (p == core)))
                def _():
                    res_copy(b, core).wait_send()


def scales(planes, count, total_k):
    return (
        -1.0 / (8.0 * math.sqrt(planes * count * (STOPS + 1))),
        1.0 / (8.0 * math.sqrt(planes * total_k)),
    )


def per_device(wavefunc, haydock, screened, coulomb, umklapp_map):
    count, _, _, planes = wavefunc.shape
    blocks = lax.axis_size("blk")
    edge = count * NV
    rows, mix = make_pieces(wavefunc, haydock)
    mix = jnp.pad(mix, ((0, 0), (0, -2 * edge % 128)))
    pieces = jnp.concatenate([rows, jnp.stack([mix, jnp.zeros_like(mix)])], axis=2)
    stop = jnp.minimum(lax.axis_index("blk"), STOPS)
    index = lax.dynamic_index_in_dim(umklapp_map, stop, 0, keepdims=False).reshape(planes, 1)
    scale_d, scale_x = scales(planes, count, count * blocks)
    lanes = pieces.shape[2]
    vmem = pl.BlockSpec(memory_space=pltpu.VMEM)
    total = pl.pallas_call(
        functools.partial(kernel, count, scale_d, scale_x),
        out_shape=jax.ShapeDtypeStruct((2 * NV, 2 * edge), jnp.float32),
        in_specs=[vmem] * 4,
        out_specs=vmem,
        scratch_shapes=[
            pltpu.VMEM((blocks, 2, 2 * edge, lanes), jnp.bfloat16),
            pltpu.VMEM((planes, planes), jnp.bfloat16),
            pltpu.VMEM((2 * edge, planes // 2), jnp.bfloat16),
            pltpu.VMEM((blocks, 2 * NV, 128), jnp.float32),
            pltpu.VMEM((2 * (STOPS + 1), 2 * NV, 128), jnp.float32),
            pltpu.VMEM((blocks, 2, planes), jnp.float32),
            pltpu.SemaphoreType.DMA((blocks,)),
            pltpu.SemaphoreType.DMA((blocks,)),
            pltpu.SemaphoreType.DMA((4, blocks)),
            pltpu.SemaphoreType.DMA((blocks, 2)),
            pltpu.SemaphoreType.DMA((2 * (STOPS + 1),)),
            pltpu.SemaphoreType.DMA((blocks,)),
            pltpu.SemaphoreType.DMA((blocks,)),
        ],
        compiler_params=pltpu.CompilerParams(
            collective_id=0, has_side_effects=True, vmem_limit_bytes=40 * 1024 * 1024
        ),
    )(pieces, screened[0], index, coulomb.reshape(1, planes))
    return unpack_result(total, count)


def per_device_general(wavefunc, haydock, screened, coulomb, umklapp_map):
    count, _, _, planes = wavefunc.shape
    blocks = lax.axis_size("blk")
    edge = count * NV
    rows, mix = make_pieces(wavefunc, haydock)
    val, cond = rows[0], rows[1]
    amp = dot_nn(mix, val)
    wide = cond.astype(jnp.float32)
    c_re, c_im, a_re, a_im = wide[:edge], wide[edge:], amp[:edge], amp[edge:]
    x_re = jnp.sum(c_re * a_re + c_im * a_im, axis=0)
    x_im = jnp.sum(c_re * a_im - c_im * a_re, axis=0)
    xs = lax.psum(jnp.stack([x_re, x_im]), "blk")
    scale_d, scale_x = scales(planes, count, count * blocks)
    y = xs * coulomb * scale_x
    v_re, v_im = val[:edge].astype(jnp.float32), val[edge:].astype(jnp.float32)
    f = jnp.concatenate([y[0] * v_re + y[1] * v_im, y[1] * v_re - y[0] * v_im], axis=0)
    current = jnp.concatenate([amp.astype(jnp.bfloat16), cond], axis=0)
    for stop in range(STOPS + 1):
        if stop > 0:
            current = lax.ppermute(current, "blk", [(i, (i + 1) % blocks) for i in range(blocks)])
        held = lax.axis_index("blk") == stop
        weight = lax.psum(jnp.where(held, screened[0], jnp.zeros_like(screened[0])), "blk")
        pick = (umklapp_map[stop][:, None] == jnp.arange(planes)[None, :]).astype(jnp.bfloat16)
        perm = dot_nt(current, pick).astype(jnp.bfloat16)
        amp_p, cond_t = perm[: 2 * edge], perm[2 * edge :].T
        turned = jnp.concatenate([amp_p[edge:], -amp_p[:edge]], axis=0)
        h_re = (dot_nn(cond_t, amp_p) * weight.astype(jnp.float32)).astype(jnp.bfloat16)
        h_im = (dot_nn(cond_t, turned) * weight.astype(jnp.float32)).astype(jnp.bfloat16)
        g_re, g_im = dot_nt(val, h_re), dot_nt(val, h_im)
        f = f + scale_d * jnp.concatenate([g_re[:edge] + g_im[edge:], g_im[:edge] - g_re[edge:]], axis=0)
    return unpack_result(fold_rows(f.astype(jnp.bfloat16), cond, count), count)


def solution(mesh):
    placed = (
        P(("grp", "blk"), None, None, None),
        P(("grp", "blk"), None),
        P(("grp", "blk"), None, None),
        P("grp"),
        P(),
    )
    body = per_device if mesh.shape["blk"] == 8 and mesh.shape["pair"] == 2 else per_device_general
    return jax.shard_map(
        body, mesh=mesh, in_specs=placed, out_specs=P(("grp", "blk"), None), check_vma=False
    )
```

profile of v0, /device:TPU:0, one launch (start us, length us, event | category | flops | bytes accessed | tf_op | source)
XLA Modules:
  0.0 71.1 jit_solution(15643010255854619947)
XLA Ops:
  0.0 0.0 copy-start
  0.0 0.0 copy-start.2
  0.0 0.8 %reshape.40 = f32[6,2,8,8]{3,2,1,0:T(8,128)S(1)} reshape(f32[6,128]{1,0:T(8,128)} %param.6) | data formatting | bytes 6144 | tf_op jit(solution)/shard_map/reshape | solution.py:30
  0.8 0.1 copy.13
  0.9 0.1 broadcast_multiply_fusion
  1.1 0.0 copy-start.3
  1.1 0.0 copy-start.1
  1.1 0.1 reshape.44
  1.2 0.1 reshape.46
  1.3 0.1 reshape.47
  1.5 0.1 fusion.8
  1.6 0.0 copy-done.2
  1.6 0.0 copy-done
  1.7 0.2 copy.14.map_ref
  1.9 0.0 copy-done.3
  1.9 0.5 copy-done.1
  2.3 67.8 %shard_map.55 = f32[16,96]{1,0:T(8,128)S(1)} custom-call(bf16[2,96,896]{2,1,0:T(8,128)(2,1)S(1)} %fusion.1.piece_ref, bf16[768,768]{1,0:T(8,128)(2,1)S(1)} %bitcast.14, s32[768,1]{1,0:T(8,128)S(1)} %copy.14.map_ref, f32[1,768]{1,0:T(1,128)S(1)} %reshape.42.coul_ref), custom_call_target="tpu_custom_call" | custom-call | tf_op jit(solution)/shard_map/pallas_call | solution.py:280
  70.2 0.1 slice_subtract_fusion
  70.2 0.1 stack.18
  70.3 0.1 stack.17
  70.4 0.7 reshape.43
  (9 shorter events, 0.2 us)
Async XLA Ops:
  0.0 1.6 %copy-start = (s32[3,768]{1,0:T(4,128)S(1)}, s32[3,768]{1,0:T(4,128)}, u32[]{:S(2)}) copy-start(s32[3,768]{1,0:T(4,128)} %param.9) | copy-start | bytes 27652
  0.0 1.6 %copy-start.2 = (bf16[6,16,2,768]{3,2,1,0:T(2,128)(2,1)S(1)}, bf16[6,16,2,768]{3,2,1,0:T(2,128)(2,1)}, u32[]{:S(2)}) copy-start(bf16[6,16,2,768]{3,2,1,0:T(2,128)(2,1)} %param.5) | copy-start | bytes 884740
  1.1 0.8 %copy-start.3 = (f32[768]{0:T(1024)S(1)}, f32[768]{0:T(1024)}, u32[]{:S(2)}) copy-start(f32[768]{0:T(1024)} %param.8) | copy-start | bytes 9220
  1.1 1.3 %copy-start.1 = (bf16[1,768,768]{2,1,0:T(8,128)(2,1)S(1)}, bf16[1,768,768]{2,1,0:T(8,128)(2,1)}, u32[]{:S(2)}) copy-start(bf16[1,768,768]{2,1,0:T(8,128)(2,1)} %param.7) | copy-start | bytes 3538948
where the time goes:
time: 71.3 us; the launch traced here: 71.1 us
  Pallas kernels  67.8 us (95%)
  local copies, waits for them, and re-layouts  2.81 us (4%)
    pallas_call x1, Pallas kernels, per_device(): pl.pallas_call(functools.partial(kernel, count, scale_d, scale_x), out_sh...  67.8 us

commit v1 on v0

--- a/solution.py
+++ b/solution.py
@@ -83,9 +83,9 @@
         xb = b % 2
         return (
             (worker & (b != me), me, 1 - p, recv_peer),
-            ((z >= 1) & (xb == x) & (zb >= z), me - 2, p, recv_near),
-            (((z == 0) & (xb == x)) | ((me == 3) & (xb == 1) & (zb >= 1)), me + 1 - 2 * x, p, recv_near),
-            ((me == 0) & (b < 2), me + 2, p, recv_near),
+            ((b == me) & (me != 0), 0, p, recv_near),
+            ((b == me) & (me != 1), 1, p, recv_near),
+            ((b == me) & (me != 2), 2, p, recv_near),
         )
 
     def copy_of(b, kind, target, core, sems):
@@ -216,13 +216,6 @@
             return carry
 
         lax.fori_loop(0, blocks, step, 0)
-
-    @pl.when(jnp.logical_not(worker))
-    def _():
-        for b in range(3, blocks):
-            @pl.when((b % 2 == x) & (b // 2 > z))
-            def _():
-                arrive(b)
 
     for d in range(1, blocks):
         src = (me + d) % blocks

time: 71.3 us -> 56.5 us (0.79)
  Pallas kernels: 67.8 us -> 53 us
    pallas_call x1, Pallas kernels: 67.8 us -> 53 us  [per_device(): pl.pallas_call(functools.partial(kernel, count, scale_d, scale_x), out_sh...]
where the time goes in v1:
time: 56.5 us; the launch traced here: 56.3 us
  Pallas kernels  53 us (94%)
  local copies, waits for them, and re-layouts  2.81 us (5%)
    pallas_call x1, Pallas kernels, per_device(): pl.pallas_call(functools.partial(kernel, count, scale_d, scale_x), out_sh...  53 us

profile of v1, /device:TPU:0, one launch (start us, length us, event | category | flops | bytes accessed | tf_op | source)
XLA Modules:
  0.0 56.3 jit_solution(7574800007572844034)
XLA Ops:
  0.0 0.0 copy-start
  0.0 0.0 copy-start.2
  0.0 0.8 %reshape.40 = f32[6,2,8,8]{3,2,1,0:T(8,128)S(1)} reshape(f32[6,128]{1,0:T(8,128)} %param.6) | data formatting | bytes 6144 | tf_op jit(solution)/shard_map/reshape | solution.py:30
  0.8 0.1 copy.13
  0.9 0.1 broadcast_multiply_fusion
  1.1 0.0 copy-start.3
  1.1 0.0 copy-start.1
  1.1 0.1 reshape.44
  1.2 0.1 reshape.46
  1.3 0.1 reshape.47
  1.5 0.1 fusion.8
  1.6 0.0 copy-done.2
  1.6 0.0 copy-done
  1.7 0.2 copy.14.map_ref
  1.9 0.0 copy-done.3
  1.9 0.5 copy-done.1
  2.3 53.0 %shard_map.55 = f32[16,96]{1,0:T(8,128)S(1)} custom-call(bf16[2,96,896]{2,1,0:T(8,128)(2,1)S(1)} %fusion.1.piece_ref, bf16[768,768]{1,0:T(8,128)(2,1)S(1)} %bitcast.14, s32[768,1]{1,0:T(8,128)S(1)} %copy.14.map_ref, f32[1,768]{1,0:T(1,128)S(1)} %reshape.42.coul_ref), custom_call_target="tpu_custom_call" | custom-call | tf_op jit(solution)/shard_map/pallas_call | solution.py:273
  55.4 0.1 slice_subtract_fusion
  55.5 0.1 stack.18
  55.5 0.1 stack.17
  55.6 0.7 %reshape.43 = f32[6,128]{1,0:T(8,128)} reshape(f32[6,2,8,8]{3,2,1,0:T(8,128)S(1)} %copy.15) | data formatting | bytes 6144 | tf_op jit(solution)/shard_map/reshape | solution.py:44
  (9 shorter events, 0.2 us)
Async XLA Ops:
  0.0 1.6 %copy-start = (s32[3,768]{1,0:T(4,128)S(1)}, s32[3,768]{1,0:T(4,128)}, u32[]{:S(2)}) copy-start(s32[3,768]{1,0:T(4,128)} %param.9) | copy-start | bytes 27652
  0.0 1.6 %copy-start.2 = (bf16[6,16,2,768]{3,2,1,0:T(2,128)(2,1)S(1)}, bf16[6,16,2,768]{3,2,1,0:T(2,128)(2,1)}, u32[]{:S(2)}) copy-start(bf16[6,16,2,768]{3,2,1,0:T(2,128)(2,1)} %param.5) | copy-start | bytes 884740
  1.1 0.8 %copy-start.3 = (f32[768]{0:T(1024)S(1)}, f32[768]{0:T(1024)}, u32[]{:S(2)}) copy-start(f32[768]{0:T(1024)} %param.8) | copy-start | bytes 9220
  1.1 1.3 %copy-start.1 = (bf16[1,768,768]{2,1,0:T(8,128)(2,1)S(1)}, bf16[1,768,768]{2,1,0:T(8,128)(2,1)}, u32[]{:S(2)}) copy-start(bf16[1,768,768]{2,1,0:T(8,128)(2,1)} %param.7) | copy-start | bytes 3538948

commit v2 on v1

--- a/solution.py
+++ b/solution.py
@@ -158,22 +158,28 @@
         ).astype(jnp.bfloat16)
 
         def step(t, carry):
-            i = jnp.where(s == 2, (t + 2) % blocks, t)
+            i = t
             b = (i + s) % blocks
-            first = jnp.where((s == 1) & (t == 0), 0, b)
+            first = jnp.where((s >= 1) & (t == 0), 0, jnp.where((s == 2) & (t == 1), 1, b))
             take = ((s == 0) & (t >= 1)) | ((s == 1) & (t <= 6)) | ((s == 2) & (t <= 5))
-            more = (s == 2) & (t == 1)
-
-            @pl.when(more)
-            def _():
-                arrive(3)
+
+            @pl.when(t == 0)
+            def _():
+                for near in range(blocks // 2):
+                    @pl.when(near != me)
+                    def _():
+                        arrive(near)
+
+            @pl.when(take & (first == blocks // 2))
+            def _():
+                for far in range(blocks // 2, blocks):
+                    arrive(far)
 
             @pl.when(take)
             def _():
-                arrive(first)
                 arrive_peer(first)
 
-            @pl.when(more)
+            @pl.when((s == 2) & (t == 1))
             def _():
                 arrive_peer(3)
 

time: 56.5 us -> 52.1 us (0.922)
  Pallas kernels: 53 us -> 48.6 us
    pallas_call x1, Pallas kernels: 53 us -> 48.6 us  [per_device(): pl.pallas_call(functools.partial(kernel, count, scale_d, scale_x), out_sh...]
where the time goes in v2:
time: 52.1 us; the launch traced here: 51.9 us
  Pallas kernels  48.6 us (93%)
  local copies, waits for them, and re-layouts  2.81 us (5%)
    pallas_call x1, Pallas kernels, per_device(): pl.pallas_call(functools.partial(kernel, count, scale_d, scale_x), out_sh...  48.6 us

profile of v2, /device:TPU:0, one launch (start us, length us, event | category | flops | bytes accessed | tf_op | source)
XLA Modules:
  0.0 51.9 jit_solution(3953193094984860548)
XLA Ops:
  0.0 0.0 copy-start
  0.0 0.0 copy-start.2
  0.0 0.8 %reshape.40 = f32[6,2,8,8]{3,2,1,0:T(8,128)S(1)} reshape(f32[6,128]{1,0:T(8,128)} %param.6) | data formatting | bytes 6144 | tf_op jit(solution)/shard_map/reshape | solution.py:30
  0.8 0.1 copy.13
  0.9 0.1 broadcast_multiply_fusion
  1.1 0.0 copy-start.3
  1.1 0.0 copy-start.1
  1.1 0.1 reshape.44
  1.2 0.1 reshape.46
  1.3 0.1 reshape.47
  1.5 0.1 fusion.8
  1.6 0.0 copy-done.2
  1.6 0.0 copy-done
  1.7 0.2 copy.14.map_ref
  1.9 0.0 copy-done.3
  1.9 0.5 copy-done.1
  2.3 48.6 %shard_map.55 = f32[16,96]{1,0:T(8,128)S(1)} custom-call(bf16[2,96,896]{2,1,0:T(8,128)(2,1)S(1)} %fusion.1.piece_ref, bf16[768,768]{1,0:T(8,128)(2,1)S(1)} %bitcast.14, s32[768,1]{1,0:T(8,128)S(1)} %copy.14.map_ref, f32[1,768]{1,0:T(1,128)S(1)} %reshape.42.coul_ref), custom_call_target="tpu_custom_call" | custom-call | tf_op jit(solution)/shard_map/pallas_call | solution.py:279
  50.9 0.1 slice_subtract_fusion
  51.0 0.1 stack.18
  51.1 0.1 stack.17
  51.2 0.7 %reshape.43 = f32[6,128]{1,0:T(8,128)} reshape(f32[6,2,8,8]{3,2,1,0:T(8,128)S(1)} %copy.15) | data formatting | bytes 6144 | tf_op jit(solution)/shard_map/reshape | solution.py:44
  (9 shorter events, 0.2 us)
Async XLA Ops:
  0.0 1.6 %copy-start = (s32[3,768]{1,0:T(4,128)S(1)}, s32[3,768]{1,0:T(4,128)}, u32[]{:S(2)}) copy-start(s32[3,768]{1,0:T(4,128)} %param.9) | copy-start | bytes 27652
  0.0 1.6 %copy-start.2 = (bf16[6,16,2,768]{3,2,1,0:T(2,128)(2,1)S(1)}, bf16[6,16,2,768]{3,2,1,0:T(2,128)(2,1)}, u32[]{:S(2)}) copy-start(bf16[6,16,2,768]{3,2,1,0:T(2,128)(2,1)} %param.5) | copy-start | bytes 884740
  1.1 0.8 %copy-start.3 = (f32[768]{0:T(1024)S(1)}, f32[768]{0:T(1024)}, u32[]{:S(2)}) copy-start(f32[768]{0:T(1024)} %param.8) | copy-start | bytes 9220
  1.1 1.3 %copy-start.1 = (bf16[1,768,768]{2,1,0:T(8,128)(2,1)S(1)}, bf16[1,768,768]{2,1,0:T(8,128)(2,1)}, u32[]{:S(2)}) copy-start(bf16[1,768,768]{2,1,0:T(8,128)(2,1)} %param.7) | copy-start | bytes 3538948

commit v3 on v2

--- a/solution.py
+++ b/solution.py
@@ -83,9 +83,9 @@
         xb = b % 2
         return (
             (worker & (b != me), me, 1 - p, recv_peer),
+            ((b == me) & (me != 2), 2, p, recv_near),
+            ((b == me) & (me != 1), 1, p, recv_near),
             ((b == me) & (me != 0), 0, p, recv_near),
-            ((b == me) & (me != 1), 1, p, recv_near),
-            ((b == me) & (me != 2), 2, p, recv_near),
         )
 
     def copy_of(b, kind, target, core, sems):

time: 52.1 us -> 44 us (0.84)
  Pallas kernels: 48.6 us -> 40.5 us
    pallas_call x1, Pallas kernels: 48.6 us -> 40.5 us  [per_device(): pl.pallas_call(functools.partial(kernel, count, scale_d, scale_x), out_sh...]
where the time goes in v3:
time: 44 us; the launch traced here: 43.8 us
  Pallas kernels  40.5 us (92%)
  local copies, waits for them, and re-layouts  2.81 us (6%)
    pallas_call x1, Pallas kernels, per_device(): pl.pallas_call(functools.partial(kernel, count, scale_d, scale_x), out_sh...  40.5 us

profile of v3, /device:TPU:0, one launch (start us, length us, event | category | flops | bytes accessed | tf_op | source)
XLA Modules:
  0.0 43.8 jit_solution(8825070637513452966)
XLA Ops:
  0.0 0.0 copy-start
  0.0 0.0 copy-start.2
  0.0 0.8 %reshape.40 = f32[6,2,8,8]{3,2,1,0:T(8,128)S(1)} reshape(f32[6,128]{1,0:T(8,128)} %param.6) | data formatting | bytes 6144 | tf_op jit(solution)/shard_map/reshape | solution.py:30
  0.8 0.1 copy.13
  0.9 0.1 broadcast_multiply_fusion
  1.1 0.0 copy-start.3
  1.1 0.0 copy-start.1
  1.1 0.1 reshape.44
  1.2 0.1 reshape.46
  1.3 0.1 reshape.47
  1.5 0.1 fusion.8
  1.6 0.0 copy-done.2
  1.6 0.0 copy-done
  1.7 0.2 copy.14.map_ref
  1.9 0.0 copy-done.3
  1.9 0.5 %copy-done.1 = bf16[1,768,768]{2,1,0:T(8,128)(2,1)S(1)} copy-done((bf16[1,768,768]{2,1,0:T(8,128)(2,1)S(1)}, bf16[1,768,768]{2,1,0:T(8,128)(2,1)}, u32[]{:S(2)}) %copy-start.1) | copy-done | bytes 1179672
  2.3 40.5 %shard_map.55 = f32[16,96]{1,0:T(8,128)S(1)} custom-call(bf16[2,96,896]{2,1,0:T(8,128)(2,1)S(1)} %fusion.1.piece_ref, bf16[768,768]{1,0:T(8,128)(2,1)S(1)} %bitcast.14, s32[768,1]{1,0:T(8,128)S(1)} %copy.14.map_ref, f32[1,768]{1,0:T(1,128)S(1)} %reshape.42.coul_ref), custom_call_target="tpu_custom_call" | custom-call | tf_op jit(solution)/shard_map/pallas_call | solution.py:279
  42.9 0.1 slice_subtract_fusion
  42.9 0.1 stack.18
  43.0 0.1 stack.17
  43.1 0.7 %reshape.43 = f32[6,128]{1,0:T(8,128)} reshape(f32[6,2,8,8]{3,2,1,0:T(8,128)S(1)} %copy.15) | data formatting | bytes 6144 | tf_op jit(solution)/shard_map/reshape | solution.py:44
  (9 shorter events, 0.2 us)
Async XLA Ops:
  0.0 1.6 %copy-start = (s32[3,768]{1,0:T(4,128)S(1)}, s32[3,768]{1,0:T(4,128)}, u32[]{:S(2)}) copy-start(s32[3,768]{1,0:T(4,128)} %param.9) | copy-start | bytes 27652
  0.0 1.6 %copy-start.2 = (bf16[6,16,2,768]{3,2,1,0:T(2,128)(2,1)S(1)}, bf16[6,16,2,768]{3,2,1,0:T(2,128)(2,1)}, u32[]{:S(2)}) copy-start(bf16[6,16,2,768]{3,2,1,0:T(2,128)(2,1)} %param.5) | copy-start | bytes 884740
  1.1 0.8 %copy-start.3 = (f32[768]{0:T(1024)S(1)}, f32[768]{0:T(1024)}, u32[]{:S(2)}) copy-start(f32[768]{0:T(1024)} %param.8) | copy-start | bytes 9220
  1.1 1.3 %copy-start.1 = (bf16[1,768,768]{2,1,0:T(8,128)(2,1)S(1)}, bf16[1,768,768]{2,1,0:T(8,128)(2,1)}, u32[]{:S(2)}) copy-start(bf16[1,768,768]{2,1,0:T(8,128)(2,1)} %param.7) | copy-start | bytes 3538948

commit v4 on v3

--- a/solution.py
+++ b/solution.py
@@ -88,10 +88,15 @@
             ((b == me) & (me != 0), 0, p, recv_near),
         )
 
-    def copy_of(b, kind, target, core, sems):
+    widths = (ubuf.shape[3], planes)
+
+    def piece(b, h):
+        return ubuf.at[b, h, :, pl.ds(0, widths[h])]
+
+    def copy_of(b, h, kind, target, core, sems):
         return pltpu.make_async_remote_copy(
-            src_ref=ubuf.at[b, p],
-            dst_ref=ubuf.at[b, p],
+            src_ref=piece(b, h),
+            dst_ref=piece(b, h),
             send_sem=send_piece.at[kind, b],
             recv_sem=sems.at[b],
             device_id=(grp, target, core),
@@ -100,22 +105,30 @@
 
     def forward(b):
         for kind, (go, target, core, sems) in enumerate(routes(b)):
-            @pl.when(go)
-            def _():
-                copy_of(b, kind, target, core, sems).start()
+            for h in range(2):
+                @pl.when(go & (p == h))
+                def _():
+                    copy_of(b, h, kind, target, core, sems).start()
 
     def drain(b):
         for kind, (go, target, core, sems) in enumerate(routes(b)):
-            @pl.when(go)
-            def _():
-                copy_of(b, kind, target, core, sems).wait_send()
+            for h in range(2):
+                @pl.when(go & (p == h))
+                def _():
+                    copy_of(b, h, kind, target, core, sems).wait_send()
 
     def arrive(b):
-        pltpu.make_async_copy(ubuf.at[b, p], ubuf.at[b, p], recv_near.at[b]).wait()
+        for h in range(2):
+            @pl.when(p == h)
+            def _():
+                pltpu.make_async_copy(piece(b, h), piece(b, h), recv_near.at[b]).wait()
         forward(b)
 
     def arrive_peer(b):
-        pltpu.make_async_copy(ubuf.at[b, 1 - p], ubuf.at[b, 1 - p], recv_peer.at[b]).wait()
+        for h in range(2):
+            @pl.when(p == 1 - h)
+            def _():
+                pltpu.make_async_copy(piece(b, h), piece(b, h), recv_peer.at[b]).wait()
 
     forward(me)
 

time: 44 us -> 42.6 us (0.968)
  Pallas kernels: 40.5 us -> 39.2 us
    pallas_call x1, Pallas kernels: 40.5 us -> 39.2 us  [per_device(): pl.pallas_call(functools.partial(kernel, count, scale_d, scale_x), out_sh...]
where the time goes in v4:
time: 42.6 us; the launch traced here: 42.5 us
  Pallas kernels  39.2 us (92%)
  local copies, waits for them, and re-layouts  2.81 us (7%)
    pallas_call x1, Pallas kernels, per_device(): pl.pallas_call(functools.partial(kernel, count, scale_d, scale_x), out_sh...  39.2 us

profile of v4, /device:TPU:0, one launch (start us, length us, event | category | flops | bytes accessed | tf_op | source)
XLA Modules:
  0.0 42.5 jit_solution(10064208318897582183)
XLA Ops:
  0.0 0.0 copy-start
  0.0 0.0 copy-start.2
  0.0 0.8 %reshape.40 = f32[6,2,8,8]{3,2,1,0:T(8,128)S(1)} reshape(f32[6,128]{1,0:T(8,128)} %param.6) | data formatting | bytes 6144 | tf_op jit(solution)/shard_map/reshape | solution.py:30
  0.8 0.1 copy.13
  0.9 0.1 broadcast_multiply_fusion
  1.1 0.0 copy-start.3
  1.1 0.0 copy-start.1
  1.1 0.1 reshape.44
  1.2 0.1 reshape.46
  1.3 0.1 reshape.47
  1.5 0.1 fusion.8
  1.6 0.0 copy-done.2
  1.6 0.0 copy-done
  1.7 0.2 copy.14.map_ref
  1.9 0.0 copy-done.3
  1.9 0.5 %copy-done.1 = bf16[1,768,768]{2,1,0:T(8,128)(2,1)S(1)} copy-done((bf16[1,768,768]{2,1,0:T(8,128)(2,1)S(1)}, bf16[1,768,768]{2,1,0:T(8,128)(2,1)}, u32[]{:S(2)}) %copy-start.1) | copy-done | bytes 1179672
  2.3 39.2 %shard_map.55 = f32[16,96]{1,0:T(8,128)S(1)} custom-call(bf16[2,96,896]{2,1,0:T(8,128)(2,1)S(1)} %fusion.1.piece_ref, bf16[768,768]{1,0:T(8,128)(2,1)S(1)} %bitcast.14, s32[768,1]{1,0:T(8,128)S(1)} %copy.14.map_ref, f32[1,768]{1,0:T(1,128)S(1)} %reshape.42.coul_ref), custom_call_target="tpu_custom_call" | custom-call | tf_op jit(solution)/shard_map/pallas_call | solution.py:292
  41.5 0.1 slice_subtract_fusion
  41.6 0.1 stack.18
  41.7 0.1 stack.17
  41.8 0.7 %reshape.43 = f32[6,128]{1,0:T(8,128)} reshape(f32[6,2,8,8]{3,2,1,0:T(8,128)S(1)} %copy.15) | data formatting | bytes 6144 | tf_op jit(solution)/shard_map/reshape | solution.py:44
  (9 shorter events, 0.2 us)
Async XLA Ops:
  0.0 1.6 %copy-start = (s32[3,768]{1,0:T(4,128)S(1)}, s32[3,768]{1,0:T(4,128)}, u32[]{:S(2)}) copy-start(s32[3,768]{1,0:T(4,128)} %param.9) | copy-start | bytes 27652
  0.0 1.6 %copy-start.2 = (bf16[6,16,2,768]{3,2,1,0:T(2,128)(2,1)S(1)}, bf16[6,16,2,768]{3,2,1,0:T(2,128)(2,1)}, u32[]{:S(2)}) copy-start(bf16[6,16,2,768]{3,2,1,0:T(2,128)(2,1)} %param.5) | copy-start | bytes 884740
  1.1 0.8 %copy-start.3 = (f32[768]{0:T(1024)S(1)}, f32[768]{0:T(1024)}, u32[]{:S(2)}) copy-start(f32[768]{0:T(1024)} %param.8) | copy-start | bytes 9220
  1.1 1.3 %copy-start.1 = (bf16[1,768,768]{2,1,0:T(8,128)(2,1)S(1)}, bf16[1,768,768]{2,1,0:T(8,128)(2,1)}, u32[]{:S(2)}) copy-start(bf16[1,768,768]{2,1,0:T(8,128)(2,1)} %param.7) | copy-start | bytes 3538948
